TPU v7x, 128 devices: a whole 4x4x4 slice. The times are simulated.
128 devices in a mesh: tm: 8 (over z, y_hi), feat: 16 (over y_lo, x, core).
Axes of the slice: x: 4, y: 4 (y_hi: 2, y_lo: 2; y = y_hi * 2 + y_lo), z: 4, core: 2. Of those that a mesh axis runs over, the one named last changes fastest.
Arguments:
- trajectory: float32 [32768, 2048], P('tm', 'feat'), may hold values from -8 to 9
Outputs:
- moments: float32 [4, 2048, 2048], P(None, 'feat', 'tm')
All inputs are finite; a program needn't handle non-finite values.
Results may differ from a plain program's by a relative error of at most 0.00035.
Values may be sent and summed in bfloat16 or wider, within the bound.
A program may use at most 128 MiB of HBM per device.

v0:
```python
import jax
import jax.numpy as jnp
from jax import lax
from jax.sharding import Mesh
from jax.sharding import PartitionSpec as P

HALO = 16
TM = ("tm_0", "tm_1")


lag_values = (0, 1, 4, 16)


def copy_for_each(array, axis):
    length = lax.axis_size(axis)
    return lax.all_to_all(
        jnp.broadcast_to(array[None], (length, *array.shape)), axis, 0, 0, tiled=True
    )


def over_copies(array, axis):
    return copy_for_each(array, axis).sum(axis=0)


def passed_along(value, axis, steps):
    count = lax.axis_size(axis)
    initial, last = (max(0, -steps), min(count, count - steps))
    return lax.ppermute(value, axis, [(source, source + steps) for source in range(initial, last)])


def summed_rows(array, axes, dim):
    for axis in axes:
        array = lax.psum_scatter(array, axis, scatter_dimension=dim, tiled=True)
    return array


def shards(trajectory):
    rows = trajectory.shape[0]
    frames = rows * lax.axis_size(TM)
    total = over_copies(jnp.sum(trajectory, axis=0), TM)
    mean = total / frames
    centered = (trajectory - mean).astype(jnp.bfloat16)
    gathered = lax.all_gather(centered, "feat", axis=1, tiled=True)
    tail = passed_along(gathered[:HALO], TM, -1)
    extended = jnp.concatenate([gathered, tail], axis=0)
    blocks = [
        lax.dot_general(
            centered,
            extended[lag : lag + rows],
            (((0,), (0,)), ((), ())),
            preferred_element_type=jnp.float32,
        )
        for lag in lag_values
    ]
    partial_sum = jnp.stack(blocks)
    summed = summed_rows(partial_sum, TM, 2)
    scales = jnp.sqrt(jnp.float32(frames) - jnp.array(lag_values, jnp.float32))
    return summed / scales[:, None, None]


def solution(mesh):
    torus = Mesh(mesh.devices.reshape(4, 2, mesh.shape["feat"]), ("tm_0", "tm_1", "feat"))
    in_specs = (P(TM, "feat"),)
    out_specs = P(None, "feat", TM)
    return jax.shard_map(
        shards, mesh=torus, in_specs=in_specs, out_specs=out_specs, check_vma=False
    )
```

profile of v0, /device:TPU:13, one launch (start us, length us, event | category | flops | bytes accessed | tf_op | source)
XLA Modules:
  0.0 242.5 jit_solution(2764542623991633967)
XLA Ops:
  6.5 0.0 all-gather.2.cloned.1.call-start
  6.5 2.1 reduce_sum.18
  8.7 13.1 %all_to_all.6 = f32[8,1,128]{2,1,0:T(1,128)S(1)} all-to-all(f32[8,1,128]{2,1,0:T(1,128)S(1)} %broadcast_in_dim.2), channel_id=1, replica_groups=mesh['tm_0'=4,'tm_1'=2,'feat'=16] {'tm_0','tm_1'}, dimensions={0} | all-to-all | bytes 8192 | tf_op jit(solution)/shard_map/all_to_all | solution.py:16
  21.8 2.7 %subtract_convert_fusion = bf16[4096,128]{1,0:T(8,128)(2,1)} fusion(f32[4096,128]{1,0:T(8,128)} %param.2, f32[128]{0:T(128)S(1)} %broadcast_multiply_fusion.1), kind=kLoop, calls=%fused_computation.11 | loop fusion | flops 1048576 | bytes 3146240 | tf_op jit(solution)/shard_map/convert_element_type | solution.py:42
  24.5 0.0 all-gather.2.cloned.1.call-update
  24.5 0.0 reduce-scatter.3.cloned.1.call-start
  24.5 97.2 %all-gather.2.cloned.1.call-done = bf16[4096,2048]{1,0:T(8,128)(2,1)} async-done(((bf16[4096,128]{1,0:T(8,128)(2,1)}), bf16[4096,2048]{1,0:T(8,128)(2,1)}) %all-gather.2.cloned.1.call-update) | async-done | bytes 16777232 | tf_op jit(solution)/shard_map/all_gather | solution.py:43
  121.8 0.0 slice-start
  121.8 1.6 slice.16
  123.4 0.0 slice-start.1
  123.4 1.5 collective-permute-start
  124.9 9.4 %constant_dynamic-update-slice_fusion.1 = bf16[4112,2048]{1,0:T(8,128)(2,1)S(1)} fusion(bf16[4096,2048]{1,0:T(8,128)(2,1)} %all-gather.2.cloned.1.call-done), kind=kLoop, calls=%fused_computation.14 | loop fusion | bytes 33554432
  134.3 0.0 slice-done
  134.3 0.0 slice-done.1
  134.3 0.0 slice-done.2
  134.3 0.0 slice-done.3
  134.4 4.6 %convolution_bitcast_fusion = f32[1,128,2048]{2,1,0:T(8,128)} fusion(bf16[4096,128]{1,0:T(8,128)(2,1)} %subtract_convert_fusion, bf16[4096,2048]{1,0:T(8,128)(2,1)S(1)} %bitcast.15), kind=kOutput, calls=%fused_computation.9 | convolution fusion | flops 2147483648 | bytes 18874368 | tf_op jit(solution)/shard_map/dot_general | solution.py:47
  139.0 0.0 collective-permute-done
  139.0 0.0 copy-start
  139.0 3.7 %fusion.9 = f32[1,128,2048]{2,1,0:T(8,128)S(1)} fusion(bf16[4096,128]{1,0:T(8,128)(2,1)} %subtract_convert_fusion, bf16[4112,2048]{1,0:T(8,128)(2,1)S(1)} %constant_dynamic-update-slice_fusion), kind=kOutput, calls=%fused_computation.8 | convolution fusion | flops 2147483648 | bytes 18874368 | tf_op jit(solution)/shard_map/dot_general | solution.py:47
  142.7 0.0 copy-done
  142.7 6.1 %fusion.12 = f32[1,128,2048]{2,1,0:T(8,128)} fusion(bf16[4096,128]{1,0:T(8,128)(2,1)S(1)} %copy-done, bf16[4112,2048]{1,0:T(8,128)(2,1)S(1)} %constant_dynamic-update-slice_fusion), kind=kOutput, calls=%fused_computation.10 | convolution fusion | flops 2147483648 | bytes 18874368 | tf_op jit(solution)/shard_map/dot_general | solution.py:47
  148.8 6.1 %fusion.6 = f32[1,128,2048]{2,1,0:T(8,128)} fusion(bf16[4096,128]{1,0:T(8,128)(2,1)S(1)} %copy-done, bf16[4112,2048]{1,0:T(8,128)(2,1)S(1)} %constant_dynamic-update-slice_fusion), kind=kOutput, calls=%fused_computation.7 | convolution fusion | flops 2147483648 | bytes 18874368 | tf_op jit(solution)/shard_map/dot_general | solution.py:47
  154.9 0.0 copy-done.1
  154.9 3.9 %pad_maximum_fusion = f32[4,128,2048]{2,1,0:T(8,128)} fusion(f32[1,128,2048]{2,1,0:T(8,128)S(1)} %fusion.9, f32[1,128,2048]{2,1,0:T(8,128)} %fusion.12, f32[1,128,2048]{2,1,0:T(8,128)} %fusion.6, f32[1,128,2048]{2,1,0:T(8,128)S(1)} %copy-done.1), kind=kLoop, calls=%fused_computation.6 | loop fusion | flops 3145728 | bytes 8388608 | tf_op jit(solution)/shard_map/stack | solution.py:55
  158.8 0.0 reduce-scatter.3.cloned.1.call-update
  158.8 0.0 reduce-scatter.5.cloned.1.call-start
  158.8 49.7 %reduce-scatter.3.cloned.1.call-done = f32[4,128,512]{2,1,0:T(8,128)} async-done(((f32[4,128,2048]{2,1,0:T(8,128)}), f32[4,128,512]{2,1,0:T(8,128)}) %reduce-scatter.3.cloned.1.call-update) | async-done | bytes 1048592 | tf_op jit(solution)/shard_map/reduce_scatter | solution.py:33
  208.5 0.0 reduce-scatter.5.cloned.1.call-update
  208.5 25.5 %reduce-scatter.5.cloned.1.call-done = f32[4,128,256]{2,1,0:T(8,128)} async-done(((f32[4,128,512]{2,1,0:T(8,128)}), f32[4,128,256]{2,1,0:T(8,128)}) %reduce-scatter.5.cloned.1.call-update) | async-done | bytes 524304 | tf_op jit(solution)/shard_map/reduce_scatter | solution.py:33
  234.0 0.0 copy-done.2
  234.0 1.9 broadcast_multiply_fusion
  (9 shorter events, 0.0 us)
Async XLA Ops:
  6.5 115.2 %all-gather.2.cloned.1.call-start = ((), (), s32[]{:S(2)}) async-start(), calls=%async_computation.3 | async-start | bytes 17825792 | tf_op jit(solution)/shard_map/all_gather | solution.py:43
  24.5 184.0 %reduce-scatter.3.cloned.1.call-start = ((), (), s32[]{:S(2)}) async-start(), calls=%async_computation.4 | async-start | bytes 5242880 | tf_op jit(solution)/shard_map/reduce_scatter | solution.py:33
  121.8 12.6 %slice-start = ((s8[16777216]{0:T(1024)(128)(4,1)}), s8[4194304]{0:T(1024)(128)(4,1)S(1)}, s32[]{:S(2)}) async-start(s8[16777216]{0:T(1024)(128)(4,1)} %bitcast.14), calls=%async_computation.6 | async-start | bytes 8388608
  123.4 10.9 %slice-start.1 = ((s8[16777216]{0:T(1024)(128)(4,1)}), s8[4194304]{0:T(1024)(128)(4,1)S(1)}, s32[]{:S(2)}) async-start(s8[16777216]{0:T(1024)(128)(4,1)} %bitcast.14), calls=%async_computation.7 | async-start | bytes 8388608
  123.4 10.9 %slice-start.2 = ((s8[16777216]{0:T(1024)(128)(4,1)}), s8[4194304]{0:T(1024)(128)(4,1)S(1)}, s32[]{:S(2)}) async-start(s8[16777216]{0:T(1024)(128)(4,1)} %bitcast.14), calls=%async_computation.8 | async-start | bytes 8388608
  123.4 11.0 %slice-start.3 = ((s8[16777216]{0:T(1024)(128)(4,1)}), s8[4194304]{0:T(1024)(128)(4,1)S(1)}, s32[]{:S(2)}) async-start(s8[16777216]{0:T(1024)(128)(4,1)} %bitcast.14), calls=%async_computation.9 | async-start | bytes 8388608
  123.4 15.6 %collective-permute-start = (bf16[16,2048]{1,0:T(8,128)(2,1)}, bf16[16,2048]{1,0:T(8,128)(2,1)S(1)}, u32[]{:S(2)}, u32[]{:S(2)}) collective-permute-start(bf16[16,2048]{1,0:T(8,128)(2,1)} %slice.16), channel_id=1, source_target_pairs={{16,0},{32,16},{48,32},{64,48},{80,64},{96,80},{112,96},{17,1},{33... | collective-permute-start | bytes 196616 | tf_op jit(solution)/shard_map/ppermute | solution.py:28
  139.0 3.7 %copy-start = (bf16[4096,128]{1,0:T(8,128)(2,1)S(1)}, bf16[4096,128]{1,0:T(8,128)(2,1)}, u32[]{:S(2)}) copy-start(bf16[4096,128]{1,0:T(8,128)(2,1)} %subtract_convert_fusion) | copy-start | bytes 3145732
  148.8 6.1 %copy-start.1 = (f32[1,128,2048]{2,1,0:T(8,128)S(1)}, f32[1,128,2048]{2,1,0:T(8,128)}, u32[]{:S(2)}) copy-start(f32[1,128,2048]{2,1,0:T(8,128)} %convolution_bitcast_fusion) | copy-start | bytes 3145732
  148.8 85.2 %copy-start.2 = (f32[4]{0:T(128)S(1)}, f32[4]{0:T(128)}, u32[]{:S(2)}) copy-start(f32[4]{0:T(128)} %constant.13) | copy-start | bytes 52
  158.8 75.2 %reduce-scatter.5.cloned.1.call-start = ((), (), s32[]{:S(2)}) async-start(), calls=%async_computation.5 | async-start | bytes 1572864 | tf_op jit(solution)/shard_map/reduce_scatter | solution.py:33
Sparse Core Ops, SparseCore 0:
  24.6 97.1 all-gather.1
  158.9 49.5 reduce-scatter.2
  211.0 22.9 reduce-scatter.4
where the time goes:
time: 245 us; the launch traced here: 242 us
  waiting for transfers between devices  172 us (70%)
  matrix products  20.5 us (8%)
  between operations  13.2 us (5%)
  blocking collectives  13.1 us (5%)
  local copies, waits for them, and re-layouts  11 us (4%)
  other arithmetic  10.6 us (4%)
    all_gather x1, waiting for transfers between devices, shards(): gathered = lax.all_gather(centered, 'feat', axis=1, tiled=True)  97.2 us
    reduce_scatter x2, waiting for transfers between devices, summed_rows(): array = lax.psum_scatter(array, axis, scatter_dimension=dim, tiled=True)  75.1 us
    dot_general x4, matrix products, shards(): lax.dot_general(centered, extended[lag:lag + rows], (((0,), (0,)), ((), (...  20.5 us
    all_to_all x1, blocking collectives, copy_for_each(): lax.all_to_all(jnp.broadcast_to(array[None], (length, *array.shape)), axi...  13.1 us
    unnamed x15, local copies, waits for them, and re-layouts  9.39 us
  transfers between devices with their start and end apart: 4, of which 3 were waited for; matrix products, arithmetic and copies ran while one was open for 6% of the time, Pallas kernels for 0%

commit v1 on v0

v1 whole, which is shorter than its diff:
```python
import functools
import math

import jax
import jax.numpy as jnp
from jax import lax
from jax.experimental import pallas as pl
from jax.experimental.pallas import tpu as pltpu
from jax.sharding import PartitionSpec as P

MESH = pl.DeviceIdType.MESH
LAGS = (0, 1, 4, 16)
HALO = 16
PARTS = 4


def device(x, y, z, c):
    return (z * 2 + y // 2, ((y % 2) * 4 + x) * 2 + c)


def kernel(
    x_ref, o_ref, sums, halo, slabs, cols, lagged, prod, recv,
    s_sum, r_sum, s_halo, r_halo, s_y, r_y, s_x, r_x, s_sib, r_sib, s_out, r_out,
):
    rows = x_ref.shape[0]
    part = rows // PARTS
    tm, feat = lax.axis_index("tm"), lax.axis_index("feat")
    c, x, a = feat % 2, (feat // 2) % 4, feat // 8
    z, h = tm // 2, tm % 2
    y = h * 2 + a
    driver = c == h
    step = 1 - 2 * c
    other = 1 - c
    ahead, behind = (y + step + 4) % 4, (y - step + 4) % 4
    across = (y + 2) % 4
    left, right, far = (x + 3) % 4, (x + 1) % 4, (x + 2) % 4

    barrier = pltpu.get_barrier_semaphore()
    place = y * 4 + z
    peers = [device(x, ((place + i) % 16) // 4, (place + i) % 4, c) for i in range(1, 16)]
    peers += [device(x, y, z, other), device(left, y, z, c), device(right, y, z, c)]
    for peer in peers:
        pl.semaphore_signal(barrier, inc=1, device_id=peer, device_id_type=MESH)

    total = jnp.zeros((8, 128), jnp.float32)
    for i in range(8):
        piece = x_ref[pl.ds(i * (rows // 8), rows // 8), :]
        total = total + jnp.sum(piece.reshape(rows // 64, 8, 128), axis=0)
    sums[tm] = total
    pl.semaphore_wait(barrier, len(peers))

    def sum_copy(slot, peer, i):
        return pltpu.make_async_remote_copy(
            src_ref=sums.at[slot], dst_ref=sums.at[slot], send_sem=s_sum.at[i],
            recv_sem=r_sum.at[slot], device_id=(peer, feat), device_id_type=MESH)

    def halo_copy(peer):
        return pltpu.make_async_remote_copy(
            src_ref=x_ref.at[pl.ds(rows - HALO, HALO)], dst_ref=halo, send_sem=s_halo,
            recv_sem=r_halo, device_id=(peer, feat), device_id_type=MESH)

    for i in range(1, 8):
        sum_copy(tm, (tm + i) % 8, i).start()

    @pl.when(tm < 7)
    def _():
        halo_copy(tm + 1).start()

    @pl.when(tm > 0)
    def _():
        halo_copy(tm - 1).wait_recv()

    @pl.when(tm == 0)
    def _():
        halo[...] = jnp.zeros_like(halo)

    for i in range(1, 8):
        sum_copy((tm + i) % 8, (tm + i) % 8, i).wait_recv()
    total = sums[0]
    for i in range(1, 8):
        total = total + sums[i]
    mean = jnp.sum(total, axis=0, keepdims=True) / (8.0 * rows)

    before = jnp.where(tm > 0, halo[...] - mean, 0.0)
    slabs[y, pl.ds(0, HALO), :] = before.astype(jnp.bfloat16)

    def centre(i, carry):
        at = pl.multiple_of(i * 512, 512)
        value = x_ref[pl.ds(at, 512), :] - mean
        slabs[y, pl.ds(pl.multiple_of(at + HALO, HALO), 512), :] = value.astype(jnp.bfloat16)
        return carry

    lax.fori_loop(0, rows // 512, centre, 0)

    def y_copy(phase, j, slab, target):
        at, size = (0, part + HALO) if j == 0 else (part * j + HALO, part)
        ref = slabs.at[slab, pl.ds(at, size)]
        return pltpu.make_async_remote_copy(
            src_ref=ref, dst_ref=ref, send_sem=s_y.at[phase, j], recv_sem=r_y.at[phase, j],
            device_id=device(x, target, z, c), device_id_type=MESH)

    def half(q):
        return h if q == 0 else 1 - h

    def x_copy(q, kind, j, owner, target):
        ref = cols.at[half(q), owner, :, pl.ds(part * j, part)]
        return pltpu.make_async_remote_copy(
            src_ref=ref, dst_ref=ref, send_sem=s_x.at[q, kind, j], recv_sem=r_x.at[q, kind, j],
            device_id=device(target, y, z, c), device_id_type=MESH)

    def sib_copy(q, kind, j):
        owner = (x, left, right, far)[kind]
        ref = cols.at[half(q), owner, :, pl.ds(part * j, part)]
        return pltpu.make_async_remote_copy(
            src_ref=ref, dst_ref=ref, send_sem=s_sib.at[q, kind, j], recv_sem=r_sib.at[q, kind, j],
            device_id=device(x, y, z, other), device_id_type=MESH)

    def send_own(q, j):
        slab = y if q == 0 else across
        value = slabs[slab, pl.ds(HALO + part * j, part), :]
        cols[half(q), x, :, pl.ds(part * j, part)] = value.T
        x_copy(q, 0, j, x, right).start()
        x_copy(q, 1, j, x, left).start()
        sib_copy(q, 0, j).start()

    def pass_neighbours(q, j):
        x_copy(q, 0, j, left, left).wait_recv()
        if j < PARTS // 2:
            x_copy(q, 2, j, left, right).start()
        sib_copy(q, 1, j).start()
        x_copy(q, 1, j, right, right).wait_recv()
        if j >= PARTS // 2:
            x_copy(q, 2, j, right, left).start()
        sib_copy(q, 2, j).start()

    def pass_far(q, j):
        x_copy(q, 2, j, far, left).wait_recv()
        sib_copy(q, 3, j).start()

    def take(q, kinds):
        @pl.when(jnp.logical_not(driver))
        def _():
            for kind in kinds:
                for j in range(PARTS):
                    sib_copy(q, kind, j).wait_recv()

    def shift(slab, j):
        def body(i, carry):
            at = pl.multiple_of(part * j + i * 256, 256)
            raw = slabs[slab, pl.ds(at, 256 + HALO), :].astype(jnp.float32)
            for k, lag in enumerate(LAGS):
                moved = raw if lag == 0 else pltpu.roll(raw, lag, 0)
                lagged[slab, pl.ds(at, 256), 128 * k:128 * (k + 1)] = (
                    moved[HALO:, :].astype(jnp.bfloat16))
            return carry

        lax.fori_loop(0, part // 256, body, 0)

    def multiply(slab, owners, first):
        def body(n, carry):
            lanes = pl.ds(pl.multiple_of(n * 256, 256), 256)
            lhs = jnp.concatenate([cols[slab // 2, owner] for owner in owners], axis=0)
            out = jnp.dot(lhs, lagged[slab, :, lanes], preferred_element_type=jnp.float32)
            for m, owner in enumerate(owners):
                block = out[128 * m:128 * (m + 1)]
                if not first:
                    block = prod[slab % 2, owner, :, lanes] + block
                prod[slab % 2, owner, :, lanes] = block
            return carry

        lax.fori_loop(0, 2, body, 0)

    for j in range(PARTS):
        y_copy(0, j, y, ahead).start()

    @pl.when(driver)
    def _():
        for j in range(PARTS):
            send_own(0, j)

    for j in range(PARTS):
        shift(y, j)

    for j in range(PARTS):
        y_copy(0, j, behind, behind).wait_recv()
        y_copy(1, j, behind, ahead).start()

        @pl.when(driver)
        def _():
            pass_neighbours(0, j)

        shift(behind, j)

    for j in range(PARTS):
        y_copy(1, j, across, behind).wait_recv()

        @pl.when(driver)
        def _():
            send_own(1, j)
            pass_far(0, j)

        if j == 1:
            for i in range(PARTS):
                y_copy(2, i, y, behind).start()
        shift(across, j)

    everyone = (x, left, right, far)
    take(0, (0, 1, 2, 3))
    multiply(y, everyone, True)

    for j in range(PARTS):
        y_copy(2, j, ahead, ahead).wait_recv()

        @pl.when(driver)
        def _():
            pass_neighbours(1, j)

        shift(ahead, j)

    twin = y + 1 - 2 * a
    multiply(twin, everyone, True)

    @pl.when(driver)
    def _():
        for j in range(PARTS):
            pass_far(1, j)

    take(1, (0, 1, 2, 3))

    def out_copy(row, owner):
        ty, tz = 2 * (owner % 2) + row, 2 * a + owner // 2
        return ty, tz, pltpu.make_async_remote_copy(
            src_ref=prod.at[row, owner], dst_ref=recv.at[tm], send_sem=s_out.at[row, owner],
            recv_sem=r_out.at[tm], device_id=device(x, ty, tz, c), device_id_type=MESH)

    def send_out(row):
        for owner in range(4):
            ty, tz, copy = out_copy(row, owner)
            here = jnp.logical_and(ty == y, tz == z)

            @pl.when(here)
            def _():
                pltpu.make_async_copy(prod.at[row, owner], recv.at[tm], r_out.at[tm]).start()

            @pl.when(jnp.logical_not(here))
            def _():
                copy.start()

    multiply(across, everyone, False)
    send_out(a)
    multiply((twin + 2) % 4, everyone, False)
    send_out(1 - a)

    for cut in range(2):
        for block in range(4):
            slot = 2 * block + cut
            pltpu.make_async_copy(prod.at[0, 0], recv.at[slot], r_out.at[slot]).wait()
        for k, lag in enumerate(LAGS):
            lanes = slice(128 * k, 128 * (k + 1))
            value = recv[cut, :, lanes]
            for block in range(1, 4):
                value = value + recv[2 * block + cut, :, lanes]
            o_ref[k, :, 128 * cut:128 * (cut + 1)] = value.T * (1.0 / math.sqrt(8 * rows - lag))

    for i in range(1, 8):
        sum_copy(tm, (tm + i) % 8, i).wait_send()

    @pl.when(tm < 7)
    def _():
        halo_copy(tm + 1).wait_send()

    for j in range(PARTS):
        y_copy(0, j, y, ahead).wait_send()
        y_copy(1, j, behind, ahead).wait_send()
        y_copy(2, j, y, behind).wait_send()

    @pl.when(driver)
    def _():
        for q in range(2):
            for j in range(PARTS):
                for kind in range(3):
                    x_copy(q, kind, j, x, right).wait_send()
                for kind in range(4):
                    sib_copy(q, kind, j).wait_send()

    for row in range(2):
        for owner in range(4):
            ty, tz, copy = out_copy(row, owner)

            @pl.when(jnp.logical_not(jnp.logical_and(ty == y, tz == z)))
            def _():
                copy.wait_send()


def block(trajectory):
    rows = trajectory.shape[0]
    return pl.pallas_call(
        kernel,
        out_shape=jax.ShapeDtypeStruct((4, 128, 256), jnp.float32),
        in_specs=[pl.BlockSpec(memory_space=pltpu.VMEM)],
        out_specs=pl.BlockSpec(memory_space=pltpu.VMEM),
        scratch_shapes=[
            pltpu.VMEM((8, 8, 128), jnp.float32),
            pltpu.VMEM((HALO, 128), jnp.float32),
            pltpu.VMEM((4, rows + HALO, 128), jnp.bfloat16),
            pltpu.VMEM((2, 4, 128, rows), jnp.bfloat16),
            pltpu.VMEM((4, rows, 512), jnp.bfloat16),
            pltpu.VMEM((2, 4, 128, 512), jnp.float32),
            pltpu.VMEM((8, 128, 512), jnp.float32),
            pltpu.SemaphoreType.DMA((8,)),
            pltpu.SemaphoreType.DMA((8,)),
            pltpu.SemaphoreType.DMA,
            pltpu.SemaphoreType.DMA,
            pltpu.SemaphoreType.DMA((3, PARTS)),
            pltpu.SemaphoreType.DMA((3, PARTS)),
            pltpu.SemaphoreType.DMA((2, 3, PARTS)),
            pltpu.SemaphoreType.DMA((2, 3, PARTS)),
            pltpu.SemaphoreType.DMA((2, 4, PARTS)),
            pltpu.SemaphoreType.DMA((2, 4, PARTS)),
            pltpu.SemaphoreType.DMA((2, 4)),
            pltpu.SemaphoreType.DMA((8,)),
        ],
        compiler_params=pltpu.CompilerParams(
            collective_id=0, has_side_effects=True, vmem_limit_bytes=52 << 20),
        cost_estimate=pl.CostEstimate(
            flops=2 * rows * 128 * 2048 * 4, bytes_accessed=3 << 20, transcendentals=0),
    )(trajectory)


def solution(mesh):
    return jax.shard_map(
        block, mesh=mesh, in_specs=(P("tm", "feat"),), out_specs=P(None, "feat", "tm"),
        check_vma=False)
```

time: 245 us -> 107 us (0.44)
  waiting for transfers between devices: 172 us -> 0 us
  Pallas kernels: 0 us -> 106 us
  matrix products: 20.5 us -> 0 us
  between operations: 13.2 us -> 0.01 us
  blocking collectives: 13.1 us -> 0 us
  other arithmetic: 10.6 us -> 0 us
  local copies, waits for them, and re-layouts: 11 us -> 0.8 us
    pallas_call x0 -> x1, Pallas kernels: none -> 106 us  [block(): pl.pallas_call(kernel, out_shape=jax.ShapeDtypeStruct((4, 128, 256), jnp....]
    all_gather x1 -> x0, waiting for transfers between devices: 97.2 us -> none  [shards(): gathered = lax.all_gather(centered, 'feat', axis=1, tiled=True)]
    reduce_scatter x2 -> x0, waiting for transfers between devices: 75.1 us -> none  [summed_rows(): array = lax.psum_scatter(array, axis, scatter_dimension=dim, tiled=True)]
    dot_general x4 -> x0, matrix products: 20.5 us -> none  [shards(): lax.dot_general(centered, extended[lag:lag + rows], (((0,), (0,)), ((), (...]
    all_to_all x1 -> x0, blocking collectives: 13.1 us -> none  [copy_for_each(): lax.all_to_all(jnp.broadcast_to(array[None], (length, *array.shape)), axi...]
    unnamed x15 -> x1, local copies, waits for them, and re-layouts: 9.39 us -> 0.8 us
    another operation x1 -> x0, other arithmetic: 3.86 us -> none  [shards(): partial_sum = jnp.stack(blocks)]
    convert_element_type x1 -> x0, other arithmetic: 2.67 us -> none  [shards(): centered = (trajectory - mean).astype(jnp.bfloat16)]
  transfers between devices with their start and end apart: 4 -> 0, of which waited for: 3 -> 0; matrix products, arithmetic and copies ran while one was open for 6% -> 0% of each run, Pallas kernels for 0% -> 0%
where the time goes in v1:
time: 107 us
  Pallas kernels  106 us (99%)
    pallas_call x1, Pallas kernels, block(): pl.pallas_call(kernel, out_shape=jax.ShapeDtypeStruct((4, 128, 256), jnp....  106 us

profile of v1, /device:TPU:13, one launch (start us, length us, event | category | flops | bytes accessed | tf_op | source)
XLA Modules:
  0.0 106.9 jit_solution(6867451415201441054)
XLA Ops:
  0.0 106.1 %shard_map.17 = f32[4,128,256]{2,1,0:T(8,128)S(1)} custom-call(f32[4096,128]{1,0:T(8,128)} %x_ref.1), custom_call_target="tpu_custom_call" | custom-call | flops 8589934592 | bytes 3145728 | tf_op jit(solution)/shard_map/pallas_call | solution.py:297
  106.1 0.8 copy.3

commit v2 on v1

--- a/solution.py
+++ b/solution.py
@@ -19,10 +19,11 @@
 
 
 def kernel(
-    x_ref, o_ref, sums, halo, slabs, cols, lagged, prod, recv,
-    s_sum, r_sum, s_halo, r_halo, s_y, r_y, s_x, r_x, s_sib, r_sib, s_out, r_out,
+    x_hbm, o_ref, x_ref, sums, halo, slabs, cols, lagged, prod, terms, owned, final,
+    s_in, s_sum, r_sum, s_halo, r_halo, s_y, r_y, s_x, r_x, s_sib, r_sib,
+    s_term, r_term, s_out, r_out,
 ):
-    rows = x_ref.shape[0]
+    rows = x_hbm.shape[0]
     part = rows // PARTS
     tm, feat = lax.axis_index("tm"), lax.axis_index("feat")
     c, x, a = feat % 2, (feat // 2) % 4, feat // 8
@@ -35,19 +36,32 @@
     across = (y + 2) % 4
     left, right, far = (x + 3) % 4, (x + 1) % 4, (x + 2) % 4
 
+    fetch = pltpu.make_async_copy(x_hbm, x_ref, s_in)
+    fetch.start()
+
     barrier = pltpu.get_barrier_semaphore()
-    place = y * 4 + z
-    peers = [device(x, ((place + i) % 16) // 4, (place + i) % 4, c) for i in range(1, 16)]
-    peers += [device(x, y, z, other), device(left, y, z, c), device(right, y, z, c)]
-    for peer in peers:
+
+    def greet(*peer):
         pl.semaphore_signal(barrier, inc=1, device_id=peer, device_id_type=MESH)
 
+    for i in range(1, 8):
+        greet((tm + i) % 8, feat)
+    for target in (ahead, behind):
+        greet(*device(x, target, z, c))
+    greet(*device(x, y, z, other))
+
+    @pl.when(driver)
+    def _():
+        for target in (left, right):
+            greet(*device(target, y, z, c))
+
+    fetch.wait()
     total = jnp.zeros((8, 128), jnp.float32)
     for i in range(8):
         piece = x_ref[pl.ds(i * (rows // 8), rows // 8), :]
         total = total + jnp.sum(piece.reshape(rows // 64, 8, 128), axis=0)
     sums[tm] = total
-    pl.semaphore_wait(barrier, len(peers))
+    pl.semaphore_wait(barrier, jnp.where(driver, 12, 10))
 
     def sum_copy(slot, peer, i):
         return pltpu.make_async_remote_copy(
@@ -84,13 +98,14 @@
     before = jnp.where(tm > 0, halo[...] - mean, 0.0)
     slabs[y, pl.ds(0, HALO), :] = before.astype(jnp.bfloat16)
 
-    def centre(i, carry):
-        at = pl.multiple_of(i * 512, 512)
-        value = x_ref[pl.ds(at, 512), :] - mean
-        slabs[y, pl.ds(pl.multiple_of(at + HALO, HALO), 512), :] = value.astype(jnp.bfloat16)
-        return carry
-
-    lax.fori_loop(0, rows // 512, centre, 0)
+    def centre(j):
+        def body(i, carry):
+            at = pl.multiple_of(part * j + i * 256, 256)
+            value = x_ref[pl.ds(at, 256), :] - mean
+            slabs[y, pl.ds(at + HALO, 256), :] = value.astype(jnp.bfloat16)
+            return carry
+
+        lax.fori_loop(0, part // 256, body, 0)
 
     def y_copy(phase, j, slab, target):
         at, size = (0, part + HALO) if j == 0 else (part * j + HALO, part)
@@ -125,11 +140,11 @@
 
     def pass_neighbours(q, j):
         x_copy(q, 0, j, left, left).wait_recv()
-        if j < PARTS // 2:
+        if j % 2 == 0:
             x_copy(q, 2, j, left, right).start()
         sib_copy(q, 1, j).start()
         x_copy(q, 1, j, right, right).wait_recv()
-        if j >= PARTS // 2:
+        if j % 2 == 1:
             x_copy(q, 2, j, right, left).start()
         sib_copy(q, 2, j).start()
 
@@ -162,20 +177,62 @@
             lhs = jnp.concatenate([cols[slab // 2, owner] for owner in owners], axis=0)
             out = jnp.dot(lhs, lagged[slab, :, lanes], preferred_element_type=jnp.float32)
             for m, owner in enumerate(owners):
-                block = out[128 * m:128 * (m + 1)]
-                if not first:
-                    block = prod[slab % 2, owner, :, lanes] + block
-                prod[slab % 2, owner, :, lanes] = block
+                for i in range(2):
+                    block = out[128 * m:128 * (m + 1), 128 * i:128 * (i + 1)]
+                    if not first:
+                        block = prod[slab % 2, owner, 2 * n + i] + block
+                    prod[slab % 2, owner, 2 * n + i] = block
             return carry
 
         lax.fori_loop(0, 2, body, 0)
 
-    for j in range(PARTS):
-        y_copy(0, j, y, ahead).start()
-
-    @pl.when(driver)
-    def _():
-        for j in range(PARTS):
+    def term_copy(row, owner, i):
+        target = (z + i) % 4
+        return pltpu.make_async_remote_copy(
+            src_ref=prod.at[row, owner, target], dst_ref=terms.at[i - 1, row, owner],
+            send_sem=s_term.at[i - 1, row, owner], recv_sem=r_term.at[i - 1, row, owner],
+            device_id=device(x, y, target, c), device_id_type=MESH)
+
+    def send_terms(row, owners):
+        for owner in owners:
+            for i in (2, 1, 3):
+                term_copy(row, owner, i).start()
+
+    def out_copy(row, owner):
+        ty, tz = 2 * (owner % 2) + row, 2 * a + owner // 2
+        copy = pltpu.make_async_remote_copy(
+            src_ref=owned.at[row, owner], dst_ref=final.at[tm], send_sem=s_out.at[row, owner],
+            recv_sem=r_out.at[tm], device_id=device(x, ty, tz, c), device_id_type=MESH)
+        return jnp.logical_and(ty == y, tz == z), copy
+
+    def send_out(row, owners):
+        for owner in owners:
+            value = prod[row, owner, z]
+            for i in range(1, 4):
+                term_copy(row, owner, i).wait_recv()
+                value = value + terms[i - 1, row, owner]
+            owned[row, owner] = value
+            here, copy = out_copy(row, owner)
+
+            @pl.when(here)
+            def _():
+                pltpu.make_async_copy(owned.at[row, owner], final.at[tm], r_out.at[tm]).start()
+
+            @pl.when(jnp.logical_not(here))
+            def _():
+                copy.start()
+
+    everyone = (x, left, right, far)
+    twin = y + 1 - 2 * a
+    opposite = (twin + 2) % 4
+
+    for j in range(PARTS):
+        centre(j)
+        if j < 2:
+            y_copy(0, j, y, ahead).start()
+
+        @pl.when(driver)
+        def _():
             send_own(0, j)
 
     for j in range(PARTS):
@@ -184,6 +241,8 @@
     for j in range(PARTS):
         y_copy(0, j, behind, behind).wait_recv()
         y_copy(1, j, behind, ahead).start()
+        if j + 2 < PARTS:
+            y_copy(0, j + 2, y, ahead).start()
 
         @pl.when(driver)
         def _():
@@ -199,14 +258,16 @@
             send_own(1, j)
             pass_far(0, j)
 
-        if j == 1:
+        if j == 2:
             for i in range(PARTS):
                 y_copy(2, i, y, behind).start()
         shift(across, j)
 
-    everyone = (x, left, right, far)
     take(0, (0, 1, 2, 3))
     multiply(y, everyone, True)
+    take(1, (0,))
+    multiply(across, (x,), False)
+    send_terms(a, (x,))
 
     for j in range(PARTS):
         y_copy(2, j, ahead, ahead).wait_recv()
@@ -217,50 +278,34 @@
 
         shift(ahead, j)
 
-    twin = y + 1 - 2 * a
+    take(1, (1, 2))
+    multiply(across, (left, right), False)
+    send_terms(a, (left, right))
     multiply(twin, everyone, True)
+    multiply(opposite, (left, right), False)
+    send_terms(1 - a, (left, right))
 
     @pl.when(driver)
     def _():
         for j in range(PARTS):
             pass_far(1, j)
 
-    take(1, (0, 1, 2, 3))
-
-    def out_copy(row, owner):
-        ty, tz = 2 * (owner % 2) + row, 2 * a + owner // 2
-        return ty, tz, pltpu.make_async_remote_copy(
-            src_ref=prod.at[row, owner], dst_ref=recv.at[tm], send_sem=s_out.at[row, owner],
-            recv_sem=r_out.at[tm], device_id=device(x, ty, tz, c), device_id_type=MESH)
-
-    def send_out(row):
-        for owner in range(4):
-            ty, tz, copy = out_copy(row, owner)
-            here = jnp.logical_and(ty == y, tz == z)
-
-            @pl.when(here)
-            def _():
-                pltpu.make_async_copy(prod.at[row, owner], recv.at[tm], r_out.at[tm]).start()
-
-            @pl.when(jnp.logical_not(here))
-            def _():
-                copy.start()
-
-    multiply(across, everyone, False)
-    send_out(a)
-    multiply((twin + 2) % 4, everyone, False)
-    send_out(1 - a)
+    take(1, (3,))
+    multiply(across, (far,), False)
+    send_terms(a, (far,))
+    multiply(opposite, (far, x), False)
+    send_terms(1 - a, (far, x))
+    send_out(a, (x, left, right))
+    send_out(1 - a, (left, right))
+    send_out(a, (far,))
+    send_out(1 - a, (far, x))
 
     for cut in range(2):
-        for block in range(4):
-            slot = 2 * block + cut
-            pltpu.make_async_copy(prod.at[0, 0], recv.at[slot], r_out.at[slot]).wait()
         for k, lag in enumerate(LAGS):
-            lanes = slice(128 * k, 128 * (k + 1))
-            value = recv[cut, :, lanes]
-            for block in range(1, 4):
-                value = value + recv[2 * block + cut, :, lanes]
-            o_ref[k, :, 128 * cut:128 * (cut + 1)] = value.T * (1.0 / math.sqrt(8 * rows - lag))
+            slot = 2 * k + cut
+            pltpu.make_async_copy(owned.at[0, 0], final.at[slot], r_out.at[slot]).wait()
+            o_ref[k, :, 128 * cut:128 * (cut + 1)] = (
+                final[slot].T * (1.0 / math.sqrt(8 * rows - lag)))
 
     for i in range(1, 8):
         sum_copy(tm, (tm + i) % 8, i).wait_send()
@@ -285,9 +330,11 @@
 
     for row in range(2):
         for owner in range(4):
-            ty, tz, copy = out_copy(row, owner)
-
-            @pl.when(jnp.logical_not(jnp.logical_and(ty == y, tz == z)))
+            for i in range(1, 4):
+                term_copy(row, owner, i).wait_send()
+            here, copy = out_copy(row, owner)
+
+            @pl.when(jnp.logical_not(here))
             def _():
                 copy.wait_send()
 
@@ -297,16 +344,20 @@
     return pl.pallas_call(
         kernel,
         out_shape=jax.ShapeDtypeStruct((4, 128, 256), jnp.float32),
-        in_specs=[pl.BlockSpec(memory_space=pltpu.VMEM)],
+        in_specs=[pl.BlockSpec(memory_space=pl.ANY)],
         out_specs=pl.BlockSpec(memory_space=pltpu.VMEM),
         scratch_shapes=[
+            pltpu.VMEM((rows, 128), jnp.float32),
             pltpu.VMEM((8, 8, 128), jnp.float32),
             pltpu.VMEM((HALO, 128), jnp.float32),
             pltpu.VMEM((4, rows + HALO, 128), jnp.bfloat16),
             pltpu.VMEM((2, 4, 128, rows), jnp.bfloat16),
             pltpu.VMEM((4, rows, 512), jnp.bfloat16),
-            pltpu.VMEM((2, 4, 128, 512), jnp.float32),
-            pltpu.VMEM((8, 128, 512), jnp.float32),
+            pltpu.VMEM((2, 4, 4, 128, 128), jnp.float32),
+            pltpu.VMEM((3, 2, 4, 128, 128), jnp.float32),
+            pltpu.VMEM((2, 4, 128, 128), jnp.float32),
+            pltpu.VMEM((8, 128, 128), jnp.float32),
+            pltpu.SemaphoreType.DMA,
             pltpu.SemaphoreType.DMA((8,)),
             pltpu.SemaphoreType.DMA((8,)),
             pltpu.SemaphoreType.DMA,
@@ -317,6 +368,8 @@
             pltpu.SemaphoreType.DMA((2, 3, PARTS)),
             pltpu.SemaphoreType.DMA((2, 4, PARTS)),
             pltpu.SemaphoreType.DMA((2, 4, PARTS)),
+            pltpu.SemaphoreType.DMA((3, 2, 4)),
+            pltpu.SemaphoreType.DMA((3, 2, 4)),
             pltpu.SemaphoreType.DMA((2, 4)),
             pltpu.SemaphoreType.DMA((8,)),
         ],

time: 107 us -> 86.1 us (0.80)
  the two profiles are of different devices: /device:TPU:13 before, /device:TPU:26 now
where the time goes in v2:
time: 86.1 us; the launch traced here: 86 us
  Pallas kernels  85.2 us (99%)
    pallas_call x1, Pallas kernels, block(): pl.pallas_call(kernel, out_shape=jax.ShapeDtypeStruct((4, 128, 256), jnp....  85.2 us

profile of v2, /device:TPU:26, one launch (start us, length us, event | category | flops | bytes accessed | tf_op | source)
XLA Modules:
  0.0 86.0 jit_solution(13801745129374771537)
XLA Ops:
  0.0 85.2 %shard_map.17 = f32[4,128,256]{2,1,0:T(8,128)S(1)} custom-call(f32[4096,128]{1,0:T(8,128)} %x_hbm.1), custom_call_target="tpu_custom_call" | custom-call | flops 8589934592 | bytes 3145728 | tf_op jit(solution)/shard_map/pallas_call | solution.py:344
  85.2 0.8 copy.3

commit v3 on v2

--- a/solution.py
+++ b/solution.py
@@ -19,7 +19,7 @@
 
 
 def kernel(
-    x_hbm, o_ref, x_ref, sums, halo, slabs, cols, lagged, prod, terms, owned, final,
+    x_hbm, o_ref, x_ref, sums, halo, slabs, cols, lagged, prod, terms, owned,
     s_in, s_sum, r_sum, s_halo, r_halo, s_y, r_y, s_x, r_x, s_sib, r_sib,
     s_term, r_term, s_out, r_out,
 ):
@@ -30,10 +30,9 @@
     z, h = tm // 2, tm % 2
     y = h * 2 + a
     driver = c == h
-    step = 1 - 2 * c
     other = 1 - c
-    ahead, behind = (y + step + 4) % 4, (y - step + 4) % 4
-    across = (y + 2) % 4
+    twin = y + 1 - 2 * a
+    opposite, across = (twin + 2) % 4, (y + 2) % 4
     left, right, far = (x + 3) % 4, (x + 1) % 4, (x + 2) % 4
 
     fetch = pltpu.make_async_copy(x_hbm, x_ref, s_in)
@@ -46,7 +45,7 @@
 
     for i in range(1, 8):
         greet((tm + i) % 8, feat)
-    for target in (ahead, behind):
+    for target in (twin, opposite):
         greet(*device(x, target, z, c))
     greet(*device(x, y, z, other))
 
@@ -107,12 +106,16 @@
 
         lax.fori_loop(0, part // 256, body, 0)
 
-    def y_copy(phase, j, slab, target):
+    def y_copy(kind, group, j, slab, target):
         at, size = (0, part + HALO) if j == 0 else (part * j + HALO, part)
         ref = slabs.at[slab, pl.ds(at, size)]
         return pltpu.make_async_remote_copy(
-            src_ref=ref, dst_ref=ref, send_sem=s_y.at[phase, j], recv_sem=r_y.at[phase, j],
+            src_ref=ref, dst_ref=ref, send_sem=s_y.at[group, j], recv_sem=r_y.at[kind, j],
             device_id=device(x, target, z, c), device_id_type=MESH)
+
+    def arrived(kind, j):
+        slab = (twin, opposite, across)[kind]
+        y_copy(kind, 0, j, slab, twin).wait_recv()
 
     def half(q):
         return h if q == 0 else 1 - h
@@ -138,26 +141,26 @@
         x_copy(q, 1, j, x, left).start()
         sib_copy(q, 0, j).start()
 
-    def pass_neighbours(q, j):
+    def neighbours(q, j):
         x_copy(q, 0, j, left, left).wait_recv()
+        sib_copy(q, 1, j).start()
+        x_copy(q, 1, j, right, right).wait_recv()
+        sib_copy(q, 2, j).start()
+
+    def pass_on(q, j):
         if j % 2 == 0:
             x_copy(q, 2, j, left, right).start()
-        sib_copy(q, 1, j).start()
-        x_copy(q, 1, j, right, right).wait_recv()
-        if j % 2 == 1:
+        else:
             x_copy(q, 2, j, right, left).start()
-        sib_copy(q, 2, j).start()
 
     def pass_far(q, j):
         x_copy(q, 2, j, far, left).wait_recv()
         sib_copy(q, 3, j).start()
 
     def take(q, kinds):
-        @pl.when(jnp.logical_not(driver))
-        def _():
-            for kind in kinds:
-                for j in range(PARTS):
-                    sib_copy(q, kind, j).wait_recv()
+        for kind in kinds:
+            for j in range(PARTS):
+                sib_copy(q, kind, j).wait_recv()
 
     def shift(slab, j):
         def body(i, carry):
@@ -200,10 +203,15 @@
 
     def out_copy(row, owner):
         ty, tz = 2 * (owner % 2) + row, 2 * a + owner // 2
+        place = o_ref.at[z, :, pl.ds(pl.multiple_of(h * 128, 128), 128)]
         copy = pltpu.make_async_remote_copy(
-            src_ref=owned.at[row, owner], dst_ref=final.at[tm], send_sem=s_out.at[row, owner],
+            src_ref=owned.at[row, owner], dst_ref=place, send_sem=s_out.at[row, owner],
             recv_sem=r_out.at[tm], device_id=device(x, ty, tz, c), device_id_type=MESH)
-        return jnp.logical_and(ty == y, tz == z), copy
+        return jnp.logical_and(ty == y, tz == z), place, copy
+
+    scale = jnp.float32(1.0 / math.sqrt(8 * rows))
+    for k in range(1, 4):
+        scale = jnp.where(z == k, jnp.float32(1.0 / math.sqrt(8 * rows - LAGS[k])), scale)
 
     def send_out(row, owners):
         for owner in owners:
@@ -211,101 +219,133 @@
             for i in range(1, 4):
                 term_copy(row, owner, i).wait_recv()
                 value = value + terms[i - 1, row, owner]
-            owned[row, owner] = value
-            here, copy = out_copy(row, owner)
+            owned[row, owner] = value.T * scale
+            here, place, copy = out_copy(row, owner)
 
             @pl.when(here)
             def _():
-                pltpu.make_async_copy(owned.at[row, owner], final.at[tm], r_out.at[tm]).start()
+                pltpu.make_async_copy(owned.at[row, owner], place, r_out.at[tm]).start()
 
             @pl.when(jnp.logical_not(here))
             def _():
                 copy.start()
 
-    everyone = (x, left, right, far)
-    twin = y + 1 - 2 * a
-    opposite = (twin + 2) % 4
-
-    for j in range(PARTS):
-        centre(j)
-        if j < 2:
-            y_copy(0, j, y, ahead).start()
-
-        @pl.when(driver)
-        def _():
+    close = (x, left, right)
+
+    @pl.when(driver)
+    def _():
+        for j in range(PARTS):
+            centre(j)
+            if j < 2:
+                y_copy(1, 0, j, y, opposite).start()
             send_own(0, j)
-
-    for j in range(PARTS):
-        shift(y, j)
-
-    for j in range(PARTS):
-        y_copy(0, j, behind, behind).wait_recv()
-        y_copy(1, j, behind, ahead).start()
-        if j + 2 < PARTS:
-            y_copy(0, j + 2, y, ahead).start()
-
-        @pl.when(driver)
-        def _():
-            pass_neighbours(0, j)
-
-        shift(behind, j)
-
-    for j in range(PARTS):
-        y_copy(1, j, across, behind).wait_recv()
-
-        @pl.when(driver)
-        def _():
+        for j in range(PARTS):
+            shift(y, j)
+        neighbours(0, 0)
+        pass_on(0, 0)
+        neighbours(0, 1)
+        pass_on(0, 1)
+        neighbours(0, 2)
+        for j in range(PARTS):
+            arrived(2, j)
             send_own(1, j)
-            pass_far(0, j)
-
-        if j == 2:
-            for i in range(PARTS):
-                y_copy(2, i, y, behind).start()
-        shift(across, j)
-
-    take(0, (0, 1, 2, 3))
-    multiply(y, everyone, True)
-    take(1, (0,))
-    multiply(across, (x,), False)
-    send_terms(a, (x,))
-
-    for j in range(PARTS):
-        y_copy(2, j, ahead, ahead).wait_recv()
-
-        @pl.when(driver)
-        def _():
-            pass_neighbours(1, j)
-
-        shift(ahead, j)
-
-    take(1, (1, 2))
-    multiply(across, (left, right), False)
-    send_terms(a, (left, right))
-    multiply(twin, everyone, True)
-    multiply(opposite, (left, right), False)
-    send_terms(1 - a, (left, right))
-
-    @pl.when(driver)
-    def _():
-        for j in range(PARTS):
-            pass_far(1, j)
-
-    take(1, (3,))
-    multiply(across, (far,), False)
-    send_terms(a, (far,))
-    multiply(opposite, (far, x), False)
-    send_terms(1 - a, (far, x))
-    send_out(a, (x, left, right))
-    send_out(1 - a, (left, right))
-    send_out(a, (far,))
-    send_out(1 - a, (far, x))
-
-    for cut in range(2):
-        for k, lag in enumerate(LAGS):
-            slot = 2 * k + cut
-            pltpu.make_async_copy(owned.at[0, 0], final.at[slot], r_out.at[slot]).wait()
-            o_ref[k, :, 128 * cut:128 * (cut + 1)] = (
-                final[slot].T * (1.0 / math.sqrt(8 * rows - lag)))
+            if j == 0:
+                neighbours(0, 3)
+            if j == 1:
+                y_copy(1, 0, 2, y, opposite).start()
+                y_copy(1, 0, 3, y, opposite).start()
+            if j >= 2:
+                pass_far(0, j - 2)
+            shift(across, j)
+        pass_on(0, 2)
+        pass_on(0, 3)
+        for j in range(PARTS):
+            y_copy(0, 1, j, y, twin).start()
+        multiply(y, close, True)
+        multiply(across, (x,), False)
+        send_terms(a, (x,))
+        for j in range(PARTS):
+            neighbours(1, j)
+            pass_on(1, j)
+        multiply(across, (left, right), False)
+        send_terms(a, (left, right))
+        pass_far(0, 2)
+        pass_far(0, 3)
+        multiply(y, (far,), True)
+        for j in range(PARTS):
+            arrived(0, j)
+            shift(twin, j)
+            if j == 1:
+                pass_far(1, 0)
+                pass_far(1, 1)
+        multiply(twin, close + (far,), True)
+        pass_far(1, 2)
+        pass_far(1, 3)
+        multiply(across, (far,), False)
+        send_terms(a, (far,))
+        for j in range(PARTS):
+            arrived(1, j)
+            shift(opposite, j)
+        multiply(opposite, close + (far,), False)
+        send_terms(1 - a, close + (far,))
+        send_out(a, close + (far,))
+        send_out(1 - a, close + (far,))
+
+    @pl.when(jnp.logical_not(driver))
+    def _():
+        for j in range(PARTS):
+            centre(j)
+            y_copy(0, 0, j, y, twin).start()
+        for j in range(PARTS):
+            shift(y, j)
+        for j in range(PARTS):
+            arrived(0, j)
+            y_copy(2, 2, j, twin, opposite).start()
+            if j < 2:
+                arrived(1, j)
+                y_copy(2, 3, j, opposite, twin).start()
+                shift(opposite, j)
+            shift(twin, j)
+        take(0, (0, 1, 2))
+        multiply(y, close, True)
+        multiply(twin, close, True)
+        for j in range(2, PARTS):
+            arrived(1, j)
+            y_copy(2, 3, j, opposite, twin).start()
+            if j == 2:
+                for i in range(PARTS):
+                    y_copy(1, 1, i, y, opposite).start()
+            shift(opposite, j)
+        take(1, (0,))
+        multiply(opposite, (x,), False)
+        send_terms(1 - a, (x,))
+        for j in range(2):
+            arrived(2, j)
+            shift(across, j)
+        take(1, (1, 2))
+        multiply(opposite, (left, right), False)
+        send_terms(1 - a, (left, right))
+        take(0, (3,))
+        multiply(y, (far,), True)
+        multiply(twin, (far,), True)
+        for j in range(2, PARTS):
+            arrived(2, j)
+            shift(across, j)
+        multiply(across, close, False)
+        send_terms(a, close)
+        take(1, (3,))
+        multiply(opposite, (far,), False)
+        send_terms(1 - a, (far,))
+        multiply(across, (far,), False)
+        send_terms(a, (far,))
+        send_out(1 - a, close)
+        send_out(a, close)
+        send_out(1 - a, (far,))
+        send_out(a, (far,))
+
+    for slot in range(8):
+        place = o_ref.at[slot // 2, :, pl.ds(128 * (slot % 2), 128)]
+        pltpu.make_async_copy(owned.at[0, 0], place, r_out.at[slot]).wait()
 
     for i in range(1, 8):
         sum_copy(tm, (tm + i) % 8, i).wait_send()
@@ -315,9 +355,8 @@
         halo_copy(tm + 1).wait_send()
 
     for j in range(PARTS):
-        y_copy(0, j, y, ahead).wait_send()
-        y_copy(1, j, behind, ahead).wait_send()
-        y_copy(2, j, y, behind).wait_send()
+        for group in range(2):
+            y_copy(0, group, j, y, twin).wait_send()
 
     @pl.when(driver)
     def _():
@@ -328,11 +367,17 @@
                 for kind in range(4):
                     sib_copy(q, kind, j).wait_send()
 
+    @pl.when(jnp.logical_not(driver))
+    def _():
+        for j in range(PARTS):
+            for group in range(2, 4):
+                y_copy(0, group, j, y, twin).wait_send()
+
     for row in range(2):
         for owner in range(4):
             for i in range(1, 4):
                 term_copy(row, owner, i).wait_send()
-            here, copy = out_copy(row, owner)
+            here, place, copy = out_copy(row, owner)
 
             @pl.when(jnp.logical_not(here))
             def _():
@@ -356,13 +401,12 @@
             pltpu.VMEM((2, 4, 4, 128, 128), jnp.float32),
             pltpu.VMEM((3, 2, 4, 128, 128), jnp.float32),
             pltpu.VMEM((2, 4, 128, 128), jnp.float32),
-            pltpu.VMEM((8, 128, 128), jnp.float32),
             pltpu.SemaphoreType.DMA,
             pltpu.SemaphoreType.DMA((8,)),
             pltpu.SemaphoreType.DMA((8,)),
             pltpu.SemaphoreType.DMA,
             pltpu.SemaphoreType.DMA,
-            pltpu.SemaphoreType.DMA((3, PARTS)),
+            pltpu.SemaphoreType.DMA((4, PARTS)),
             pltpu.SemaphoreType.DMA((3, PARTS)),
             pltpu.SemaphoreType.DMA((2, 3, PARTS)),
             pltpu.SemaphoreType.DMA((2, 3, PARTS)),

time: 86.1 us -> 80.8 us (0.938)
  the two profiles are of different devices: /device:TPU:26 before, /device:TPU:30 now
where the time goes in v3:
time: 80.8 us; the launch traced here: 80.7 us
  Pallas kernels  79.9 us (99%)
    pallas_call x1, Pallas kernels, block(): pl.pallas_call(kernel, out_shape=jax.ShapeDtypeStruct((4, 128, 256), jnp....  79.9 us

profile of v3, /device:TPU:30, one launch (start us, length us, event | category | flops | bytes accessed | tf_op | source)
XLA Modules:
  0.0 80.7 jit_solution(2049368293807701585)
XLA Ops:
  0.0 79.9 %shard_map.17 = f32[4,128,256]{2,1,0:T(8,128)S(1)} custom-call(f32[4096,128]{1,0:T(8,128)} %x_hbm.1), custom_call_target="tpu_custom_call" | custom-call | flops 8589934592 | bytes 3145728 | tf_op jit(solution)/shard_map/pallas_call | solution.py:389
  79.9 0.8 copy.3

commit v4 on v3

--- a/solution.py
+++ b/solution.py
@@ -15,7 +15,7 @@
 
 
 def device(x, y, z, c):
-    return (z * 2 + y // 2, ((y % 2) * 4 + x) * 2 + c)
+    return (z * 2 + (y >> 1), ((y & 1) * 4 + x) * 2 + c)
 
 
 def kernel(
@@ -26,14 +26,14 @@
     rows = x_hbm.shape[0]
     part = rows // PARTS
     tm, feat = lax.axis_index("tm"), lax.axis_index("feat")
-    c, x, a = feat % 2, (feat // 2) % 4, feat // 8
-    z, h = tm // 2, tm % 2
+    c, x, a = feat & 1, (feat >> 1) & 3, feat >> 3
+    z, h = tm >> 1, tm & 1
     y = h * 2 + a
     driver = c == h
     other = 1 - c
     twin = y + 1 - 2 * a
-    opposite, across = (twin + 2) % 4, (y + 2) % 4
-    left, right, far = (x + 3) % 4, (x + 1) % 4, (x + 2) % 4
+    opposite, across = (twin + 2) & 3, (y + 2) & 3
+    left, right, far = (x + 3) & 3, (x + 1) & 3, (x + 2) & 3
 
     fetch = pltpu.make_async_copy(x_hbm, x_ref, s_in)
     fetch.start()
@@ -44,7 +44,7 @@
         pl.semaphore_signal(barrier, inc=1, device_id=peer, device_id_type=MESH)
 
     for i in range(1, 8):
-        greet((tm + i) % 8, feat)
+        greet((tm + i) & 7, feat)
     for target in (twin, opposite):
         greet(*device(x, target, z, c))
     greet(*device(x, y, z, other))
@@ -73,7 +73,7 @@
             recv_sem=r_halo, device_id=(peer, feat), device_id_type=MESH)
 
     for i in range(1, 8):
-        sum_copy(tm, (tm + i) % 8, i).start()
+        sum_copy(tm, (tm + i) & 7, i).start()
 
     @pl.when(tm < 7)
     def _():
@@ -88,7 +88,7 @@
         halo[...] = jnp.zeros_like(halo)
 
     for i in range(1, 8):
-        sum_copy((tm + i) % 8, (tm + i) % 8, i).wait_recv()
+        sum_copy((tm + i) & 7, (tm + i) & 7, i).wait_recv()
     total = sums[0]
     for i in range(1, 8):
         total = total + sums[i]
@@ -128,7 +128,7 @@
 
     def sib_copy(q, kind, j):
         owner = (x, left, right, far)[kind]
-        ref = cols.at[half(q), owner, :, pl.ds(part * j, part)]
+        ref = cols.at[half(q), owner, :, pl.ds(2 * part * j, 2 * part)]
         return pltpu.make_async_remote_copy(
             src_ref=ref, dst_ref=ref, send_sem=s_sib.at[q, kind, j], recv_sem=r_sib.at[q, kind, j],
             device_id=device(x, y, z, other), device_id_type=MESH)
@@ -139,13 +139,15 @@
         cols[half(q), x, :, pl.ds(part * j, part)] = value.T
         x_copy(q, 0, j, x, right).start()
         x_copy(q, 1, j, x, left).start()
-        sib_copy(q, 0, j).start()
+        if j % 2:
+            sib_copy(q, 0, j // 2).start()
 
     def neighbours(q, j):
         x_copy(q, 0, j, left, left).wait_recv()
-        sib_copy(q, 1, j).start()
         x_copy(q, 1, j, right, right).wait_recv()
-        sib_copy(q, 2, j).start()
+        if j % 2:
+            sib_copy(q, 1, j // 2).start()
+            sib_copy(q, 2, j // 2).start()
 
     def pass_on(q, j):
         if j % 2 == 0:
@@ -155,11 +157,12 @@
 
     def pass_far(q, j):
         x_copy(q, 2, j, far, left).wait_recv()
-        sib_copy(q, 3, j).start()
+        if j % 2:
+            sib_copy(q, 3, j // 2).start()
 
     def take(q, kinds):
         for kind in kinds:
-            for j in range(PARTS):
+            for j in range(PARTS // 2):
                 sib_copy(q, kind, j).wait_recv()
 
     def shift(slab, j):
@@ -174,23 +177,25 @@
 
         lax.fori_loop(0, part // 256, body, 0)
 
-    def multiply(slab, owners, first):
+    def multiply(slab, owners, first, parts=None):
+        at = pl.ds(0, rows) if parts is None else pl.ds(part * parts[0], part * len(parts))
+
         def body(n, carry):
             lanes = pl.ds(pl.multiple_of(n * 256, 256), 256)
-            lhs = jnp.concatenate([cols[slab // 2, owner] for owner in owners], axis=0)
-            out = jnp.dot(lhs, lagged[slab, :, lanes], preferred_element_type=jnp.float32)
+            lhs = jnp.concatenate([cols[slab >> 1, owner, :, at] for owner in owners], axis=0)
+            out = jnp.dot(lhs, lagged[slab, at, lanes], preferred_element_type=jnp.float32)
             for m, owner in enumerate(owners):
                 for i in range(2):
                     block = out[128 * m:128 * (m + 1), 128 * i:128 * (i + 1)]
                     if not first:
-                        block = prod[slab % 2, owner, 2 * n + i] + block
-                    prod[slab % 2, owner, 2 * n + i] = block
+                        block = prod[slab & 1, owner, 2 * n + i] + block
+                    prod[slab & 1, owner, 2 * n + i] = block
             return carry
 
         lax.fori_loop(0, 2, body, 0)
 
     def term_copy(row, owner, i):
-        target = (z + i) % 4
+        target = (z + i) & 3
         return pltpu.make_async_remote_copy(
             src_ref=prod.at[row, owner, target], dst_ref=terms.at[i - 1, row, owner],
             send_sem=s_term.at[i - 1, row, owner], recv_sem=r_term.at[i - 1, row, owner],
@@ -202,7 +207,7 @@
                 term_copy(row, owner, i).start()
 
     def out_copy(row, owner):
-        ty, tz = 2 * (owner % 2) + row, 2 * a + owner // 2
+        ty, tz = 2 * (owner & 1) + row, 2 * a + (owner >> 1)
         place = o_ref.at[z, :, pl.ds(pl.multiple_of(h * 128, 128), 128)]
         copy = pltpu.make_async_remote_copy(
             src_ref=owned.at[row, owner], dst_ref=place, send_sem=s_out.at[row, owner],
@@ -236,8 +241,7 @@
     def _():
         for j in range(PARTS):
             centre(j)
-            if j < 2:
-                y_copy(1, 0, j, y, opposite).start()
+            y_copy(1, 0, j, y, opposite).start()
             send_own(0, j)
         for j in range(PARTS):
             shift(y, j)
@@ -251,16 +255,14 @@
             send_own(1, j)
             if j == 0:
                 neighbours(0, 3)
-            if j == 1:
-                y_copy(1, 0, 2, y, opposite).start()
-                y_copy(1, 0, 3, y, opposite).start()
+            if j == 2:
+                for i in range(PARTS):
+                    y_copy(0, 1, i, y, twin).start()
             if j >= 2:
                 pass_far(0, j - 2)
             shift(across, j)
         pass_on(0, 2)
         pass_on(0, 3)
-        for j in range(PARTS):
-            y_copy(0, 1, j, y, twin).start()
         multiply(y, close, True)
         multiply(across, (x,), False)
         send_terms(a, (x,))
@@ -283,12 +285,19 @@
         pass_far(1, 3)
         multiply(across, (far,), False)
         send_terms(a, (far,))
+        send_out(a, close)
         for j in range(PARTS):
             arrived(1, j)
             shift(opposite, j)
-        multiply(opposite, close + (far,), False)
-        send_terms(1 - a, close + (far,))
-        send_out(a, close + (far,))
+            if j == 1:
+                multiply(opposite, close + (far,), False, (0, 1))
+            if j == 2:
+                multiply(opposite, close + (far,), False, (2,))
+        multiply(opposite, (x, left), False, (3,))
+        send_terms(1 - a, (x, left))
+        multiply(opposite, (right, far), False, (3,))
+        send_terms(1 - a, (right, far))
+        send_out(a, (far,))
         send_out(1 - a, close + (far,))
 
     @pl.when(jnp.logical_not(driver))
@@ -301,45 +310,40 @@
         for j in range(PARTS):
             arrived(0, j)
             y_copy(2, 2, j, twin, opposite).start()
-            if j < 2:
-                arrived(1, j)
-                y_copy(2, 3, j, opposite, twin).start()
-                shift(opposite, j)
+            arrived(1, j)
+            y_copy(2, 3, j, opposite, twin).start()
+            shift(opposite, j)
             shift(twin, j)
+        for j in range(PARTS):
+            y_copy(1, 1, j, y, opposite).start()
         take(0, (0, 1, 2))
         multiply(y, close, True)
         multiply(twin, close, True)
-        for j in range(2, PARTS):
-            arrived(1, j)
-            y_copy(2, 3, j, opposite, twin).start()
-            if j == 2:
-                for i in range(PARTS):
-                    y_copy(1, 1, i, y, opposite).start()
-            shift(opposite, j)
+        for j in range(PARTS):
+            arrived(2, j)
+            shift(across, j)
         take(1, (0,))
         multiply(opposite, (x,), False)
         send_terms(1 - a, (x,))
-        for j in range(2):
-            arrived(2, j)
-            shift(across, j)
+        multiply(across, (x,), False)
+        send_terms(a, (x,))
         take(1, (1, 2))
         multiply(opposite, (left, right), False)
         send_terms(1 - a, (left, right))
+        multiply(across, (left, right), False)
+        send_terms(a, (left, right))
         take(0, (3,))
         multiply(y, (far,), True)
         multiply(twin, (far,), True)
-        for j in range(2, PARTS):
-            arrived(2, j)
-            shift(across, j)
-        multiply(across, close, False)
-        send_terms(a, close)
+        send_out(1 - a, (x,))
+        send_out(a, (x,))
         take(1, (3,))
         multiply(opposite, (far,), False)
         send_terms(1 - a, (far,))
         multiply(across, (far,), False)
         send_terms(a, (far,))
-        send_out(1 - a, close)
-        send_out(a, close)
+        send_out(1 - a, (left, right))
+        send_out(a, (left, right))
         send_out(1 - a, (far,))
         send_out(a, (far,))
 
@@ -348,7 +352,7 @@
         pltpu.make_async_copy(owned.at[0, 0], place, r_out.at[slot]).wait()
 
     for i in range(1, 8):
-        sum_copy(tm, (tm + i) % 8, i).wait_send()
+        sum_copy(tm, (tm + i) & 7, i).wait_send()
 
     @pl.when(tm < 7)
     def _():
@@ -364,6 +368,7 @@
             for j in range(PARTS):
                 for kind in range(3):
                     x_copy(q, kind, j, x, right).wait_send()
+            for j in range(PARTS // 2):
                 for kind in range(4):
                     sib_copy(q, kind, j).wait_send()
 
@@ -390,7 +395,7 @@
         kernel,
         out_shape=jax.ShapeDtypeStruct((4, 128, 256), jnp.float32),
         in_specs=[pl.BlockSpec(memory_space=pl.ANY)],
-        out_specs=pl.BlockSpec(memory_space=pltpu.VMEM),
+        out_specs=pl.BlockSpec(memory_space=pl.ANY),
         scratch_shapes=[
             pltpu.VMEM((rows, 128), jnp.float32),
             pltpu.VMEM((8, 8, 128), jnp.float32),
@@ -410,8 +415,8 @@
             pltpu.SemaphoreType.DMA((3, PARTS)),
             pltpu.SemaphoreType.DMA((2, 3, PARTS)),
             pltpu.SemaphoreType.DMA((2, 3, PARTS)),
-            pltpu.SemaphoreType.DMA((2, 4, PARTS)),
-            pltpu.SemaphoreType.DMA((2, 4, PARTS)),
+            pltpu.SemaphoreType.DMA((2, 4, PARTS // 2)),
+            pltpu.SemaphoreType.DMA((2, 4, PARTS // 2)),
             pltpu.SemaphoreType.DMA((3, 2, 4)),
             pltpu.SemaphoreType.DMA((3, 2, 4)),
             pltpu.SemaphoreType.DMA((2, 4)),

time: 80.8 us -> 77.1 us (0.954)
  the two profiles are of different devices: /device:TPU:30 before, /device:TPU:13 now
where the time goes in v4:
time: 77.1 us; the launch traced here: 76.9 us
  Pallas kernels  76.1 us (99%)
  local copies, waits for them, and re-layouts  0.8 us (1%)
    pallas_call x1, Pallas kernels, block(): pl.pallas_call(kernel, out_shape=jax.ShapeDtypeStruct((4, 128, 256), jnp....  76.1 us

profile of v4, /device:TPU:13, one launch (start us, length us, event | category | flops | bytes accessed | tf_op | source)
XLA Modules:
  0.0 76.9 jit_solution(11889170317343870088)
XLA Ops:
  0.0 76.1 %shard_map.17 = f32[4,128,256]{2,1,0:T(8,128)S(1)} custom-call(f32[4096,128]{1,0:T(8,128)} %x_hbm.1), custom_call_target="tpu_custom_call" | custom-call | flops 8589934592 | bytes 3145728 | tf_op jit(solution)/shard_map/pallas_call | solution.py:394
  76.2 0.8 %copy.3 = f32[4,128,256]{2,1,0:T(8,128)} copy(f32[4,128,256]{2,1,0:T(8,128)S(1)} %shard_map.17) | data formatting | bytes 1048576

commit v5 on v4

--- a/solution.py
+++ b/solution.py
@@ -43,7 +43,7 @@
     def greet(*peer):
         pl.semaphore_signal(barrier, inc=1, device_id=peer, device_id_type=MESH)
 
-    for i in range(1, 8):
+    for i in (5, 3, 4, 7, 1, 6, 2):
         greet((tm + i) & 7, feat)
     for target in (twin, opposite):
         greet(*device(x, target, z, c))
@@ -72,7 +72,7 @@
             src_ref=x_ref.at[pl.ds(rows - HALO, HALO)], dst_ref=halo, send_sem=s_halo,
             recv_sem=r_halo, device_id=(peer, feat), device_id_type=MESH)
 
-    for i in range(1, 8):
+    for i in (5, 3, 4, 7, 1, 6, 2):
         sum_copy(tm, (tm + i) & 7, i).start()
 
     @pl.when(tm < 7)
@@ -274,6 +274,7 @@
         pass_far(0, 2)
         pass_far(0, 3)
         multiply(y, (far,), True)
+        send_out(a, (x,))
         for j in range(PARTS):
             arrived(0, j)
             shift(twin, j)
@@ -285,7 +286,7 @@
         pass_far(1, 3)
         multiply(across, (far,), False)
         send_terms(a, (far,))
-        send_out(a, close)
+        send_out(a, (left, right))
         for j in range(PARTS):
             arrived(1, j)
             shift(opposite, j)
@@ -319,12 +320,12 @@
         take(0, (0, 1, 2))
         multiply(y, close, True)
         multiply(twin, close, True)
-        for j in range(PARTS):
-            arrived(2, j)
-            shift(across, j)
         take(1, (0,))
         multiply(opposite, (x,), False)
         send_terms(1 - a, (x,))
+        for j in range(PARTS):
+            arrived(2, j)
+            shift(across, j)
         multiply(across, (x,), False)
         send_terms(a, (x,))
         take(1, (1, 2))
@@ -335,21 +336,15 @@
         take(0, (3,))
         multiply(y, (far,), True)
         multiply(twin, (far,), True)
-        send_out(1 - a, (x,))
-        send_out(a, (x,))
         take(1, (3,))
         multiply(opposite, (far,), False)
         send_terms(1 - a, (far,))
         multiply(across, (far,), False)
         send_terms(a, (far,))
-        send_out(1 - a, (left, right))
-        send_out(a, (left, right))
+        send_out(1 - a, close)
+        send_out(a, close)
         send_out(1 - a, (far,))
         send_out(a, (far,))
-
-    for slot in range(8):
-        place = o_ref.at[slot // 2, :, pl.ds(128 * (slot % 2), 128)]
-        pltpu.make_async_copy(owned.at[0, 0], place, r_out.at[slot]).wait()
 
     for i in range(1, 8):
         sum_copy(tm, (tm + i) & 7, i).wait_send()
@@ -387,6 +382,10 @@
             @pl.when(jnp.logical_not(here))
             def _():
                 copy.wait_send()
+
+    for slot in range(8):
+        place = o_ref.at[slot // 2, :, pl.ds(128 * (slot % 2), 128)]
+        pltpu.make_async_copy(owned.at[0, 0], place, r_out.at[slot]).wait()
 
 
 def block(trajectory):

time: 77.1 us -> 76.3 us (0.990)
  Pallas kernels: 76.1 us -> 75.1 us
    pallas_call x1, Pallas kernels: 76.1 us -> 75.1 us  [block(): pl.pallas_call(kernel, out_shape=jax.ShapeDtypeStruct((4, 128, 256), jnp....]
where the time goes in v5:
time: 76.3 us; the launch traced here: 75.9 us
  Pallas kernels  75.1 us (98%)
  local copies, waits for them, and re-layouts  0.8 us (1%)
    pallas_call x1, Pallas kernels, block(): pl.pallas_call(kernel, out_shape=jax.ShapeDtypeStruct((4, 128, 256), jnp....  75.1 us

profile of v5, /device:TPU:13, one launch (start us, length us, event | category | flops | bytes accessed | tf_op | source)
XLA Modules:
  0.0 75.9 jit_solution(15816526393899635718)
XLA Ops:
  0.0 75.1 %shard_map.17 = f32[4,128,256]{2,1,0:T(8,128)S(1)} custom-call(f32[4096,128]{1,0:T(8,128)} %x_hbm.1), custom_call_target="tpu_custom_call" | custom-call | flops 8589934592 | bytes 3145728 | tf_op jit(solution)/shard_map/pallas_call | solution.py:393
  75.1 0.8 %copy.3 = f32[4,128,256]{2,1,0:T(8,128)} copy(f32[4,128,256]{2,1,0:T(8,128)S(1)} %shard_map.17) | data formatting | bytes 1048576

commit v6 on v5

--- a/solution.py
+++ b/solution.py
@@ -170,9 +170,11 @@
             at = pl.multiple_of(part * j + i * 256, 256)
             raw = slabs[slab, pl.ds(at, 256 + HALO), :].astype(jnp.float32)
             for k, lag in enumerate(LAGS):
-                moved = raw if lag == 0 else pltpu.roll(raw, lag, 0)
-                lagged[slab, pl.ds(at, 256), 128 * k:128 * (k + 1)] = (
-                    moved[HALO:, :].astype(jnp.bfloat16))
+                if lag % HALO == 0:
+                    moved = slabs[slab, pl.ds(at + HALO - lag, 256), :]
+                else:
+                    moved = pltpu.roll(raw, lag, 0)[HALO:, :].astype(jnp.bfloat16)
+                lagged[slab, pl.ds(at, 256), 128 * k:128 * (k + 1)] = moved
             return carry
 
         lax.fori_loop(0, part // 256, body, 0)

time: 76.3 us -> 76.3 us (level)
  no operation moved by 1% of the time
where the time goes in v6:
time: 76.3 us; the launch traced here: 75.9 us
  Pallas kernels  75.1 us (98%)
  local copies, waits for them, and re-layouts  0.8 us (1%)
    pallas_call x1, Pallas kernels, block(): pl.pallas_call(kernel, out_shape=jax.ShapeDtypeStruct((4, 128, 256), jnp....  75.1 us

profile of v6, /device:TPU:13, one launch (start us, length us, event | category | flops | bytes accessed | tf_op | source)
XLA Modules:
  0.0 75.9 jit_solution(6670985467526302535)
XLA Ops:
  0.0 75.1 %shard_map.17 = f32[4,128,256]{2,1,0:T(8,128)S(1)} custom-call(f32[4096,128]{1,0:T(8,128)} %x_hbm.1), custom_call_target="tpu_custom_call" | custom-call | flops 8589934592 | bytes 3145728 | tf_op jit(solution)/shard_map/pallas_call | solution.py:395
  75.1 0.8 %copy.3 = f32[4,128,256]{2,1,0:T(8,128)} copy(f32[4,128,256]{2,1,0:T(8,128)S(1)} %shard_map.17) | data formatting | bytes 1048576

commit v7 on v5

--- a/solution.py
+++ b/solution.py
@@ -241,8 +241,8 @@
     def _():
         for j in range(PARTS):
             centre(j)
+            send_own(0, j)
             y_copy(1, 0, j, y, opposite).start()
-            send_own(0, j)
         for j in range(PARTS):
             shift(y, j)
         neighbours(0, 0)

time: 76.3 us -> 76.4 us (level)
  no operation moved by 1% of the time
where the time goes in v7:
time: 76.4 us; the launch traced here: 76 us
  Pallas kernels  75.2 us (98%)
  local copies, waits for them, and re-layouts  0.8 us (1%)
    pallas_call x1, Pallas kernels, block(): pl.pallas_call(kernel, out_shape=jax.ShapeDtypeStruct((4, 128, 256), jnp....  75.2 us

profile of v7, /device:TPU:13, one launch (start us, length us, event | category | flops | bytes accessed | tf_op | source)
XLA Modules:
  0.0 76.0 jit_solution(4267813506725571595)
XLA Ops:
  0.0 75.2 %shard_map.17 = f32[4,128,256]{2,1,0:T(8,128)S(1)} custom-call(f32[4096,128]{1,0:T(8,128)} %x_hbm.1), custom_call_target="tpu_custom_call" | custom-call | flops 8589934592 | bytes 3145728 | tf_op jit(solution)/shard_map/pallas_call | solution.py:393
  75.2 0.8 %copy.3 = f32[4,128,256]{2,1,0:T(8,128)} copy(f32[4,128,256]{2,1,0:T(8,128)S(1)} %shard_map.17) | data formatting | bytes 1048576
